TPU v7x, 32 devices: a whole 2x2x4 slice. The times are simulated.
32 devices in a mesh: rep: 2 (over y), tp: 8 (over z, x), sub: 2 (over core).
Axes of the slice: x: 2, y: 2, z: 4, core: 2. Of those that a mesh axis runs over, the one named last changes fastest.
Arguments:
- query: bfloat16 [64, 8, 128], P(('rep', 'sub'), 'tp'), parts along dimension 0, may hold values from -6 to 6
- new_key: bfloat16 [64, 8, 128], P(('rep', 'sub'), 'tp'), parts along dimension 0, may hold values from -5 to 5
- new_value: bfloat16 [64, 8, 128], P(('rep', 'sub'), 'tp'), parts along dimension 0, may hold values from -12 to 12
- cache_keys: bfloat16 [8, 64, 192, 128], P('tp', ('rep', 'sub')), parts along dimension 1, may hold values from -6 to 6, as said below
- cache_values: bfloat16 [8, 64, 192, 128], P('tp', ('rep', 'sub')), parts along dimension 1, may hold values from -12 to 12, as said below
- lengths: int32 [64], P(('rep', 'sub')), parts along dimension 0, may hold values from 2 to 192, as said below
- out_weight: bfloat16 [1024, 16384], P(('tp', 'sub')), may hold values from -0.25 to 0.25
- residual: bfloat16 [64, 16384], P('rep', ('tp', 'sub')), parts along dimension 0, may hold values from -6 to 6
Outputs:
- stream: bfloat16 [64, 16384], P('rep'), parts along dimension 0
There are 2 independent parts, one for each index of `rep`. A program takes and returns all parts, laid end to end along the dimension named above; an argument that names none is the same for every part. Nothing has to cross between parts.
Inputs may be any that keep to these rules, and one draw needn't show every extreme that they name: `lengths`: each row's count of filled slots; some row in every draw fills all 192 slots. cache_keys[h] equals cache_keys[h2] whenever h // 8 == h2 // 8. cache_values[h] equals cache_values[h2] whenever h // 8 == h2 // 8.
All inputs are finite; a program needn't handle non-finite values.
Results may differ from a plain program's by a relative error of at most 0.0049.
Values may be sent and summed in bfloat16 or wider, within the bound.
A program may use at most 64 MiB of HBM per device.

v0:
```python
import math

import jax
import jax.numpy as jnp
from jax import lax
from jax.sharding import PartitionSpec as P

D = 16384


def per_device(query, new_key, new_value, cache_keys, cache_values, lengths, out_weight, residual):
    rows_here, heads_here, head_dim = query.shape
    slots = cache_keys.shape[2]
    scale = 1.0 / math.sqrt(head_dim)
    scores = (
        jnp.einsum("rhd,hrpd->hrp", query, cache_keys, preferred_element_type=jnp.float32) * scale
    )
    own = jnp.sum(query.astype(jnp.float32) * new_key.astype(jnp.float32), axis=-1) * scale
    own = jnp.transpose(own)
    valid = jnp.arange(slots)[None, None, :] < lengths[None, :, None]
    scores = jnp.where(valid, scores, -jnp.inf)
    top = jnp.maximum(jnp.max(scores, axis=-1), own)
    expo = jnp.exp(scores - top[:, :, None])
    expo_own = jnp.exp(own - top)
    total = jnp.sum(expo, axis=-1) + expo_own
    probs = (expo / total[:, :, None]).astype(jnp.bfloat16)
    probs_own = (expo_own / total).astype(jnp.bfloat16)
    mixed = jnp.einsum("hrp,hrpd->rhd", probs, cache_values, preferred_element_type=jnp.float32)
    mixed = mixed + jnp.transpose(probs_own).astype(jnp.float32)[:, :, None] * new_value.astype(
        jnp.float32
    )
    context = mixed.astype(jnp.bfloat16).reshape(rows_here, heads_here * head_dim)
    halves = lax.all_to_all(context, "sub", split_axis=1, concat_axis=0, tiled=True)
    all_rows = halves.shape[0]
    n_tp = lax.axis_size("tp")
    n_sub = lax.axis_size("sub")
    n_all = n_tp * n_sub
    width = D // n_all
    weight_view = out_weight.reshape(out_weight.shape[0], n_all, width)
    partial_value = jnp.einsum(
        "rk,kgc->grc", halves, weight_view, preferred_element_type=jnp.float32
    )
    arranged = partial_value.reshape(n_all, all_rows * width)
    summed = lax.psum_scatter(arranged, ("tp", "sub"), scatter_dimension=0, tiled=True)
    own_columns = summed.reshape(all_rows, width)
    updated = (residual.astype(jnp.float32) + own_columns).astype(jnp.bfloat16)
    gathered = lax.all_gather(
        updated.reshape(1, all_rows * width), ("tp", "sub"), axis=0, tiled=True
    )
    whole = jnp.transpose(gathered.reshape(n_all, all_rows, width), (1, 0, 2))
    return whole.reshape(all_rows, D)


def solution(mesh):
    return jax.shard_map(
        per_device,
        mesh=mesh,
        in_specs=(
            P(("rep", "sub"), "tp", None),
            P(("rep", "sub"), "tp", None),
            P(("rep", "sub"), "tp", None),
            P("tp", ("rep", "sub"), None, None),
            P("tp", ("rep", "sub"), None, None),
            P(("rep", "sub")),
            P(("tp", "sub"), None),
            P("rep", ("tp", "sub")),
        ),
        out_specs=P("rep", None),
        check_vma=False,
    )
```

profile of v0, /device:TPU:0, one launch (start us, length us, event | category | flops | bytes accessed | tf_op | source)
XLA Modules:
  0.0 182.8 jit_solution(2479499885166838498)
XLA Ops:
  6.5 0.9 multiply_reduce_fusion
  7.4 0.3 copy-done
  7.7 1.2 fusion.5
  8.9 0.9 fusion.10
  9.8 0.8 fusion.9
  10.6 0.7 fusion.12
  11.4 1.4 fusion.3
  12.8 0.8 add_convert_fusion.1
  13.6 0.1 all_to_all.14
  13.7 0.1 reshape.149
  13.8 3.7 %all_to_all.19 = bf16[2,2,512]{2,1,0:T(2,128)(2,1)S(1)} all-to-all(bf16[2,2,512]{2,1,0:T(2,128)(2,1)S(1)} %reshape.149), channel_id=1, replica_groups=mesh['rep'=2,'tp'=8,'sub'=2] {'sub'}, dimensions={0} | all-to-all | bytes 8192 | tf_op jit(solution)/shard_map/all_to_all | solution.py:33
  17.4 0.1 reshape.150
  17.5 2.0 %fusion = f32[32,16,1024]{2,0,1:T(8,128)S(1)} fusion(bf16[32,64,1]{1,0,2:T(8,128)(2,1)S(1)} %bitcast.58, bf16[8,16,8,1024]{3,2,1,0:T(8,128)(2,1)} %bitcast.55), kind=kOutput, calls=%fused_computation | convolution fusion | flops 67108864 | bytes 4198400 | tf_op jit(solution)/shard_map/rk,kgc->grc/dot_general | solution.py:40
  19.5 2.5 %copy.30 = f32[2,8,32,1024]{3,1,2,0:T(8,128)} copy(f32[2,8,32,1024]{3,2,1,0:T(8,128)S(1)} %bitcast.52) | data formatting | bytes 4194304
  22.1 0.0 all-gather.3.cloned.1.call-start
  22.1 0.6 copy-done.2
  22.7 0.6 dynamic-slice
  23.3 99.5 %all-reduce.3.cloned.1.call-done = f32[16,32768]{1,0:T(8,128)} async-done(((f32[16,32768]{1,0:T(8,128)}), f32[16,32768]{1,0:T(8,128)}) %all-reduce.3.cloned.1.call-update) | async-done | bytes 2097168
  122.8 2.2 %dynamic-slice_reduce_fusion = f32[32768]{0:T(1024)S(1)} fusion(f32[16,32768]{1,0:T(8,128)} %all-reduce.3.cloned.1.call-done, u32[]{:T(128)} %bitcast.16), kind=kLoop, calls=%fused_computation.7 | loop fusion | bytes 262148
  125.0 0.7 reshape.131
  125.8 40.8 %all-gather.3.cloned.1.call-done = bf16[16,1,32768]{2,1,0:T(2,128)(2,1)} async-done(((bf16[1,1,32768]{2,1,0:T(2,128)(2,1)}), bf16[16,1,32768]{2,1,0:T(2,128)(2,1)}) %all-gather.3.cloned.1.call-update) | async-done | bytes 1048592 | tf_op jit(solution)/shard_map/all_gather | solution.py:47
  166.6 7.7 %reduce.6 = bf16[16,32768]{1,0:T(8,128)(2,1)S(1)} reduce(bf16[16,1,32768]{2,1,0:T(2,128)(2,1)} %all-gather.3.cloned.1.call-done, bf16[]{:T(256)} %constant.17), dimensions={1}, to_apply=%all-gather.reduce_sub_computation | reduce | bytes 2097154 | tf_op jit(solution)/shard_map/all_gather | solution.py:47
  174.3 0.6 copy.31
  174.9 1.1 copy.29
  (12 shorter events, 0.1 us)
Async XLA Ops:
  6.5 1.2 copy-start
  6.5 116.2 %all-reduce.3.cloned.1.call-start = ((), (), s32[]{:S(2)}) async-start(), calls=%async_computation.2 | async-start | bytes 4194304
  22.1 0.7 copy-start.2
  22.1 103.0 %copy-start.1 = (bf16[32,1024]{1,0:T(8,128)(2,1)S(1)}, bf16[32,1024]{1,0:T(8,128)(2,1)}, u32[]{:S(2)}) copy-start(bf16[32,1024]{1,0:T(8,128)(2,1)} %param.15) | copy-start | bytes 196612
  22.1 144.5 %all-gather.3.cloned.1.call-start = ((), (), s32[]{:S(2)}) async-start(), calls=%async_computation.1 | async-start | bytes 2228224 | tf_op jit(solution)/shard_map/all_gather | solution.py:47
Sparse Core Ops, SparseCore 0:
  22.2 100.5 all-reduce.2
  125.9 40.6 all-gather.2
where the time goes:
time: 183 us
  waiting for transfers between devices  140 us (77%)
  between operations  13.5 us (7%)
  other arithmetic  11.9 us (7%)
  local copies, waits for them, and re-layouts  8.81 us (5%)
  matrix products  4.62 us (3%)
  blocking collectives  3.68 us (2%)
    unnamed x3, waiting for transfers between devices  99.5 us
    all_gather x1, waiting for transfers between devices, per_device(): lax.all_gather(updated.reshape(1, all_rows * width), ('tp', 'sub'), axis=...  40.8 us
    all_gather x1, other arithmetic, per_device(): lax.all_gather(updated.reshape(1, all_rows * width), ('tp', 'sub'), axis=...  7.73 us
    unnamed x13, local copies, waits for them, and re-layouts  7.63 us
    all_to_all x1, blocking collectives, per_device(): lax.all_to_all(context, 'sub', split_axis=1, concat_axis=0, tiled=True)  3.68 us
  transfers between devices with their start and end apart: 2, of which 2 were waited for; matrix products, arithmetic and copies ran while one was open for 0% of the time, Pallas kernels for 0%

commit v1 on v0

--- a/solution.py
+++ b/solution.py
@@ -1,11 +1,312 @@
+import functools
 import math
 
 import jax
 import jax.numpy as jnp
 from jax import lax
+from jax.experimental import pallas as pl
+from jax.experimental.pallas import tpu as pltpu
 from jax.sharding import PartitionSpec as P
 
 D = 16384
+INNER = 2
+MESH = pl.DeviceIdType.MESH
+
+
+def fused_kernel(
+    outer,
+    order,
+    query_ref,
+    key_ref,
+    value_ref,
+    lengths_ref,
+    residual_ref,
+    keys_hbm,
+    values_hbm,
+    weight_hbm,
+    out_ref,
+    keys,
+    values,
+    weight,
+    context,
+    x_out,
+    x_in,
+    z_out,
+    z_in,
+    totals,
+    local_sem,
+    weight_local,
+    weight_send,
+    weight_recv,
+    context_sem,
+    x_send,
+    x_recv,
+    z_send,
+    z_recv,
+    gz_send,
+    gz_recv,
+    gx_send,
+    gx_recv,
+    gs_send,
+    gs_recv,
+):
+    tp = lax.axis_index("tp")
+    sub = lax.axis_index("sub")
+    z = lax.div(tp, INNER)
+    x = lax.rem(tp, INNER)
+    rows, head_dim = query_ref.shape
+    all_rows, width = residual_ref.shape
+    depth = weight_hbm.shape[0]
+    slots = keys.shape[0] // rows
+
+    other_core = {"sub": 1 - sub}
+    other_x = {"tp": z * INNER + 1 - x}
+
+    def along(k):
+        return {"tp": lax.rem(z + k, outer) * INNER + x}
+
+    def block_at(z_at, x_at, sub_at):
+        first = ((z_at * INNER + x_at) * 2 + sub_at) * width
+        return pl.ds(pl.multiple_of(first, width), width)
+
+    barrier = pltpu.get_barrier_semaphore()
+    partners = [other_core, other_x] + [along(k) for k in range(1, outer)]
+    for partner in partners:
+        pl.semaphore_signal(barrier, inc=1, device_id=partner, device_id_type=MESH)
+
+    load_keys = pltpu.make_async_copy(keys_hbm, keys, local_sem.at[0])
+    load_values = pltpu.make_async_copy(values_hbm, values, local_sem.at[1])
+    load_keys.start()
+    load_values.start()
+
+    blocks = [(1 - x, k) for k in order] + [(x, k) for k in order]
+    mine = pl.ds(pl.multiple_of(sub * depth, depth), depth)
+    load_weight = []
+    for j, (x_at, k) in enumerate(blocks):
+        copy = pltpu.make_async_copy(
+            weight_hbm.at[:, block_at(lax.rem(z + k, outer), x_at, sub)],
+            weight.at[j, mine],
+            weight_local.at[j],
+        )
+        copy.start()
+        load_weight.append(copy)
+
+    pl.semaphore_wait(barrier, len(partners))
+
+    send_weight = []
+    for j, (x_at, k) in enumerate(blocks):
+        copy = pltpu.make_async_remote_copy(
+            src_ref=weight_hbm.at[:, block_at(lax.rem(z + k, outer), x_at, 1 - sub)],
+            dst_ref=weight.at[j, mine],
+            send_sem=weight_send.at[j],
+            recv_sem=weight_recv.at[j],
+            device_id=other_core,
+            device_id_type=MESH,
+        )
+        copy.start()
+        send_weight.append(copy)
+
+    scale = 1.0 / math.sqrt(head_dim)
+    query = query_ref[...]
+    row = lax.broadcasted_iota(jnp.int32, (rows, 1), 0)
+    filled = jnp.zeros((rows, 1), jnp.int32)
+    for r in range(rows):
+        filled = jnp.where(row == r, lengths_ref[r], filled)
+    own = (
+        jnp.sum(
+            query.astype(jnp.float32) * key_ref[...].astype(jnp.float32), axis=1, keepdims=True
+        )
+        * scale
+    )
+    load_keys.wait()
+    scores = (
+        lax.dot_general(
+            query, keys[...], (((1,), (1,)), ((), ())), preferred_element_type=jnp.float32
+        )
+        * scale
+    )
+    place = lax.broadcasted_iota(jnp.int32, scores.shape, 1) - row * slots
+    valid = (place >= 0) & (place < filled)
+    scores = jnp.where(valid, scores, -jnp.inf)
+    top = jnp.maximum(jnp.max(scores, axis=1, keepdims=True), own)
+    expo = jnp.exp(scores - top)
+    expo_own = jnp.exp(own - top)
+    total = jnp.sum(expo, axis=1, keepdims=True) + expo_own
+    probs = (expo / total).astype(jnp.bfloat16)
+    probs_own = (expo_own / total).astype(jnp.bfloat16)
+    load_values.wait()
+    mixed = jnp.dot(probs, values[...], preferred_element_type=jnp.float32)
+    mixed = mixed + probs_own.astype(jnp.float32) * value_ref[...].astype(jnp.float32)
+    my_rows = pl.ds(pl.multiple_of(sub * rows, rows), rows)
+    context[my_rows, :] = mixed.astype(jnp.bfloat16)
+    send_context = pltpu.make_async_remote_copy(
+        src_ref=context.at[my_rows],
+        dst_ref=context.at[my_rows],
+        send_sem=context_sem.at[0],
+        recv_sem=context_sem.at[1],
+        device_id=other_core,
+        device_id_type=MESH,
+    )
+    send_context.start()
+    send_context.wait_recv()
+    whole_context = context[...]
+
+    n = len(order)
+    x_copies = []
+    for j in range(n):
+        load_weight[j].wait()
+        send_weight[j].wait_recv()
+        x_out[j] = jnp.dot(
+            whole_context, weight[j], preferred_element_type=jnp.float32
+        ).astype(jnp.bfloat16)
+        copy = pltpu.make_async_remote_copy(
+            src_ref=x_out.at[j],
+            dst_ref=x_in.at[j],
+            send_sem=x_send.at[j],
+            recv_sem=x_recv.at[j],
+            device_id=other_x,
+            device_id_type=MESH,
+        )
+        copy.start()
+        x_copies.append(copy)
+    for j in range(n):
+        load_weight[n + j].wait()
+        send_weight[n + j].wait_recv()
+        totals[j] = jnp.dot(whole_context, weight[n + j], preferred_element_type=jnp.float32)
+    z_copies = {}
+    summed = None
+    for j, k in enumerate(order):
+        x_copies[j].wait_recv()
+        both = totals[j] + x_in[j].astype(jnp.float32)
+        if k == 0:
+            summed = both
+            continue
+        z_out[k - 1] = both.astype(jnp.bfloat16)
+        copy = pltpu.make_async_remote_copy(
+            src_ref=z_out.at[k - 1],
+            dst_ref=z_in.at[k - 1],
+            send_sem=z_send.at[k - 1],
+            recv_sem=z_recv.at[k - 1],
+            device_id=along(k),
+            device_id_type=MESH,
+        )
+        copy.start()
+        z_copies[k] = copy
+    summed = summed + residual_ref[...].astype(jnp.float32)
+    for k in order:
+        if k > 0:
+            z_copies[k].wait_recv()
+            summed = summed + z_in[k - 1].astype(jnp.float32)
+    here = block_at(z, x, sub)
+    out_ref[:, here] = summed.astype(jnp.bfloat16)
+
+    sent = []
+
+    def pass_on(block, device, send_sem, recv_sem):
+        copy = pltpu.make_async_remote_copy(
+            src_ref=out_ref.at[:, block],
+            dst_ref=out_ref.at[:, block],
+            send_sem=send_sem,
+            recv_sem=recv_sem,
+            device_id=device,
+            device_id_type=MESH,
+        )
+        copy.start()
+        sent.append(copy)
+        return copy
+
+    def arrived(block, send_sem, recv_sem):
+        pltpu.make_async_remote_copy(
+            src_ref=out_ref.at[:, block],
+            dst_ref=out_ref.at[:, block],
+            send_sem=send_sem,
+            recv_sem=recv_sem,
+            device_id=other_core,
+            device_id_type=MESH,
+        ).wait_recv()
+
+    hops = [0] + [k for k in order if k > 0]
+    for k in hops[1:]:
+        pass_on(here, along(k), gz_send.at[k - 1], gz_recv.at[k - 1])
+    for k in hops:
+        block = block_at(lax.rem(z + outer - k, outer), x, sub)
+        if k > 0:
+            arrived(block, gz_send.at[k - 1], gz_recv.at[k - 1])
+        pass_on(block, other_x, gx_send.at[k], gx_recv.at[k])
+        pass_on(block, other_core, gs_send.at[k], gs_recv.at[k])
+    for k in hops:
+        block = block_at(lax.rem(z + outer - k, outer), 1 - x, sub)
+        arrived(block, gx_send.at[k], gx_recv.at[k])
+        pass_on(block, other_core, gs_send.at[outer + k], gs_recv.at[outer + k])
+    for i, x_at in enumerate((x, 1 - x)):
+        for k in hops:
+            block = block_at(lax.rem(z + outer - k, outer), x_at, 1 - sub)
+            arrived(block, gs_send.at[i * outer + k], gs_recv.at[i * outer + k])
+
+    send_context.wait_send()
+    for copy in send_weight + x_copies + list(z_copies.values()) + sent:
+        copy.wait_send()
+
+
+def per_device_fused(
+    query, new_key, new_value, cache_keys, cache_values, lengths, out_weight, residual
+):
+    rows, _, head_dim = query.shape
+    slots = cache_keys.shape[2]
+    depth, columns = out_weight.shape
+    all_rows, width = residual.shape
+    outer = lax.axis_size("tp") // INNER
+    order = [2, 1, 3, 0] if outer == 4 else [k for k in range(1, outer)] + [0]
+    vmem = pl.BlockSpec(memory_space=pltpu.VMEM)
+    anywhere = pl.BlockSpec(memory_space=pl.ANY)
+    block = (all_rows, width)
+    dma = pltpu.SemaphoreType.DMA
+    return pl.pallas_call(
+        functools.partial(fused_kernel, outer, order),
+        out_shape=jax.ShapeDtypeStruct((all_rows, columns), jnp.bfloat16),
+        in_specs=[vmem] * 3
+        + [pl.BlockSpec(memory_space=pltpu.SMEM), vmem]
+        + [anywhere] * 3,
+        out_specs=vmem,
+        scratch_shapes=[
+            pltpu.VMEM((rows * slots, head_dim), jnp.bfloat16),
+            pltpu.VMEM((rows * slots, head_dim), jnp.bfloat16),
+            pltpu.VMEM((2 * outer, 2 * depth, width), jnp.bfloat16),
+            pltpu.VMEM((all_rows, head_dim), jnp.bfloat16),
+            pltpu.VMEM((outer, *block), jnp.bfloat16),
+            pltpu.VMEM((outer, *block), jnp.bfloat16),
+            pltpu.VMEM((outer - 1, *block), jnp.bfloat16),
+            pltpu.VMEM((outer - 1, *block), jnp.bfloat16),
+            pltpu.VMEM((outer, *block), jnp.float32),
+            dma((2,)),
+            dma((2 * outer,)),
+            dma((2 * outer,)),
+            dma((2 * outer,)),
+            dma((2,)),
+            dma((outer,)),
+            dma((outer,)),
+            dma((outer - 1,)),
+            dma((outer - 1,)),
+            dma((outer - 1,)),
+            dma((outer - 1,)),
+            dma((outer,)),
+            dma((outer,)),
+            dma((2 * outer,)),
+            dma((2 * outer,)),
+        ],
+        compiler_params=pltpu.CompilerParams(
+            collective_id=0, has_side_effects=True, vmem_limit_bytes=56 * 2**20
+        ),
+    )(
+        query.reshape(rows, head_dim),
+        new_key.reshape(rows, head_dim),
+        new_value.reshape(rows, head_dim),
+        lengths,
+        residual,
+        cache_keys.reshape(rows * slots, head_dim),
+        cache_values.reshape(rows * slots, head_dim),
+        out_weight,
+    )
 
 
 def per_device(query, new_key, new_value, cache_keys, cache_values, lengths, out_weight, residual):
@@ -52,8 +353,11 @@
 
 
 def solution(mesh):
+    n_tp, n_sub = mesh.shape["tp"], mesh.shape["sub"]
+    width = D // (n_tp * n_sub)
+    fused = n_sub == 2 and n_tp % INNER == 0 and 4 <= n_tp <= 16 and width % 128 == 0
     return jax.shard_map(
-        per_device,
+        per_device_fused if fused else per_device,
         mesh=mesh,
         in_specs=(
             P(("rep", "sub"), "tp", None),

time: 183 us -> 35.7 us (0.20)
  waiting for transfers between devices: 140 us -> 0 us
  Pallas kernels: 0 us -> 33.3 us
  between operations: 13.5 us -> 0.01 us
  other arithmetic: 11.9 us -> 0 us
  local copies, waits for them, and re-layouts: 8.81 us -> 2.26 us
  matrix products: 4.62 us -> 0 us
  blocking collectives: 3.68 us -> 0 us
    unnamed x3 -> x0, waiting for transfers between devices: 99.5 us -> none
    all_gather x1 -> x0, waiting for transfers between devices: 40.8 us -> none  [per_device(): lax.all_gather(updated.reshape(1, all_rows * width), ('tp', 'sub'), axis=...]
    pallas_call x0 -> x1, Pallas kernels: none -> 33.3 us  [per_device_fused(): pl.pallas_call(functools.partial(fused_kernel, outer, order), out_shape=j...]
    all_gather x1 -> x0, other arithmetic: 7.73 us -> none  [per_device(): lax.all_gather(updated.reshape(1, all_rows * width), ('tp', 'sub'), axis=...]
    unnamed x13 -> x1, local copies, waits for them, and re-layouts: 7.63 us -> 2.26 us
    dot_general x3 -> x0, matrix products: 4.62 us -> none  [the longest x1 2.01 us: per_device(): jnp.einsum('rk,kgc->grc', halves, weight_view, preferred_element_type=jnp...]
    all_to_all x1 -> x0, blocking collectives: 3.68 us -> none  [per_device(): lax.all_to_all(context, 'sub', split_axis=1, concat_axis=0, tiled=True)]
  transfers between devices with their start and end apart: 2 -> 0, of which waited for: 2 -> 0; matrix products, arithmetic and copies ran while one was open for 0% -> 0% of each run, Pallas kernels for 0% -> 0%
where the time goes in v1:
time: 35.7 us; the launch traced here: 35.5 us
  Pallas kernels  33.3 us (93%)
  local copies, waits for them, and re-layouts  2.26 us (6%)
    pallas_call x1, Pallas kernels, per_device_fused(): pl.pallas_call(functools.partial(fused_kernel, outer, order), out_shape=j...  33.3 us
    unnamed x1, local copies, waits for them, and re-layouts  2.26 us

profile of v1, /device:TPU:0, one launch (start us, length us, event | category | flops | bytes accessed | tf_op | source)
XLA Modules:
  0.0 35.5 jit_solution(15333860535432502868)
XLA Ops:
  0.0 33.3 %shard_map.82 = bf16[32,16384]{1,0:T(8,128)(2,1)} custom-call(bf16[16,128]{1,0:T(8,128)(2,1)} %bitcast.7, bf16[16,128]{1,0:T(8,128)(2,1)} %bitcast.8, bf16[16,128]{1,0:T(8,128)(2,1)} %bitcast.9, s32[16]{0:T(128)} %lengths_ref.1, bf16[32,1024]{1,0:T(8,128)(2,1)} %residual_ref.1, bf16[3072,128]{1,0:T(8,128)(2,1)} %bitcast.5, bf16[3072,128]{1,0:T(8,128)(2,1)} %bitcast.6, ...), custom_call_target="tpu_custom_call" | custom-call | tf_op jit(solution)/shard_map/pallas_call | solution.py:264
  33.3 2.3 %copy.10 = bf16[32,16384]{1,0:T(8,128)(2,1)} copy(bf16[32,16384]{1,0:T(8,128)(2,1)} %shard_map.82) | data formatting | bytes 2097152

commit v2 on v1

--- a/solution.py
+++ b/solution.py
@@ -10,6 +10,7 @@
 
 D = 16384
 INNER = 2
+PARTS = 2
 MESH = pl.DeviceIdType.MESH
 
 
@@ -91,6 +92,25 @@
         copy.start()
         load_weight.append(copy)
 
+    scale = 1.0 / math.sqrt(head_dim)
+    query = query_ref[...]
+    row = lax.broadcasted_iota(jnp.int32, (rows, 1), 0)
+    filled = jnp.zeros((rows, 1), jnp.int32)
+    for r in range(rows):
+        filled = jnp.where(row == r, lengths_ref[r], filled)
+    own = (
+        jnp.sum(
+            query.astype(jnp.float32) * key_ref[...].astype(jnp.float32), axis=1, keepdims=True
+        )
+        * scale
+    )
+    load_keys.wait()
+    scores = (
+        lax.dot_general(
+            query, keys[...], (((1,), (1,)), ((), ())), preferred_element_type=jnp.float32
+        )
+        * scale
+    )
     pl.semaphore_wait(barrier, len(partners))
 
     send_weight = []
@@ -106,25 +126,6 @@
         copy.start()
         send_weight.append(copy)
 
-    scale = 1.0 / math.sqrt(head_dim)
-    query = query_ref[...]
-    row = lax.broadcasted_iota(jnp.int32, (rows, 1), 0)
-    filled = jnp.zeros((rows, 1), jnp.int32)
-    for r in range(rows):
-        filled = jnp.where(row == r, lengths_ref[r], filled)
-    own = (
-        jnp.sum(
-            query.astype(jnp.float32) * key_ref[...].astype(jnp.float32), axis=1, keepdims=True
-        )
-        * scale
-    )
-    load_keys.wait()
-    scores = (
-        lax.dot_general(
-            query, keys[...], (((1,), (1,)), ((), ())), preferred_element_type=jnp.float32
-        )
-        * scale
-    )
     place = lax.broadcasted_iota(jnp.int32, scores.shape, 1) - row * slots
     valid = (place >= 0) & (place < filled)
     scores = jnp.where(valid, scores, -jnp.inf)
@@ -152,99 +153,100 @@
     whole_context = context[...]
 
     n = len(order)
-    x_copies = []
-    for j in range(n):
-        load_weight[j].wait()
-        send_weight[j].wait_recv()
-        x_out[j] = jnp.dot(
-            whole_context, weight[j], preferred_element_type=jnp.float32
-        ).astype(jnp.bfloat16)
+    part = width // PARTS
+    parts = [slice(p * part, (p + 1) * part) for p in range(PARTS)]
+    sent = []
+
+    def send(src, dst, device, send_sem, recv_sem):
         copy = pltpu.make_async_remote_copy(
-            src_ref=x_out.at[j],
-            dst_ref=x_in.at[j],
-            send_sem=x_send.at[j],
-            recv_sem=x_recv.at[j],
-            device_id=other_x,
+            src_ref=src,
+            dst_ref=dst,
+            send_sem=send_sem,
+            recv_sem=recv_sem,
+            device_id=device,
             device_id_type=MESH,
         )
         copy.start()
-        x_copies.append(copy)
+        sent.append(copy)
+        return copy
+
+    x_copies = {}
+    for p, cols in enumerate(parts):
+        for j in range(n):
+            if p == 0:
+                load_weight[j].wait()
+                send_weight[j].wait_recv()
+            x_out[j, :, cols] = jnp.dot(
+                whole_context, weight[j, :, cols], preferred_element_type=jnp.float32
+            ).astype(jnp.bfloat16)
+            x_copies[p, j] = send(
+                x_out.at[j, :, cols],
+                x_in.at[j, :, cols],
+                other_x,
+                x_send.at[p, j],
+                x_recv.at[p, j],
+            )
     for j in range(n):
         load_weight[n + j].wait()
         send_weight[n + j].wait_recv()
         totals[j] = jnp.dot(whole_context, weight[n + j], preferred_element_type=jnp.float32)
     z_copies = {}
-    summed = None
-    for j, k in enumerate(order):
-        x_copies[j].wait_recv()
-        both = totals[j] + x_in[j].astype(jnp.float32)
-        if k == 0:
-            summed = both
-            continue
-        z_out[k - 1] = both.astype(jnp.bfloat16)
-        copy = pltpu.make_async_remote_copy(
-            src_ref=z_out.at[k - 1],
-            dst_ref=z_in.at[k - 1],
-            send_sem=z_send.at[k - 1],
-            recv_sem=z_recv.at[k - 1],
-            device_id=along(k),
-            device_id_type=MESH,
-        )
-        copy.start()
-        z_copies[k] = copy
-    summed = summed + residual_ref[...].astype(jnp.float32)
-    for k in order:
-        if k > 0:
-            z_copies[k].wait_recv()
-            summed = summed + z_in[k - 1].astype(jnp.float32)
-    here = block_at(z, x, sub)
-    out_ref[:, here] = summed.astype(jnp.bfloat16)
-
-    sent = []
-
-    def pass_on(block, device, send_sem, recv_sem):
-        copy = pltpu.make_async_remote_copy(
-            src_ref=out_ref.at[:, block],
-            dst_ref=out_ref.at[:, block],
-            send_sem=send_sem,
-            recv_sem=recv_sem,
-            device_id=device,
-            device_id_type=MESH,
-        )
-        copy.start()
-        sent.append(copy)
-        return copy
-
-    def arrived(block, send_sem, recv_sem):
-        pltpu.make_async_remote_copy(
-            src_ref=out_ref.at[:, block],
-            dst_ref=out_ref.at[:, block],
-            send_sem=send_sem,
-            recv_sem=recv_sem,
-            device_id=other_core,
-            device_id_type=MESH,
-        ).wait_recv()
-
-    hops = [0] + [k for k in order if k > 0]
-    for k in hops[1:]:
-        pass_on(here, along(k), gz_send.at[k - 1], gz_recv.at[k - 1])
-    for k in hops:
-        block = block_at(lax.rem(z + outer - k, outer), x, sub)
-        if k > 0:
-            arrived(block, gz_send.at[k - 1], gz_recv.at[k - 1])
-        pass_on(block, other_x, gx_send.at[k], gx_recv.at[k])
-        pass_on(block, other_core, gs_send.at[k], gs_recv.at[k])
-    for k in hops:
-        block = block_at(lax.rem(z + outer - k, outer), 1 - x, sub)
-        arrived(block, gx_send.at[k], gx_recv.at[k])
-        pass_on(block, other_core, gs_send.at[outer + k], gs_recv.at[outer + k])
-    for i, x_at in enumerate((x, 1 - x)):
+    for p, cols in enumerate(parts):
+        for j, k in enumerate(order):
+            x_copies[p, j].wait_recv()
+            both = totals[j, :, cols] + x_in[j, :, cols].astype(jnp.float32)
+            if k == 0:
+                totals[j, :, cols] = both
+                continue
+            z_out[k - 1, :, cols] = both.astype(jnp.bfloat16)
+            z_copies[p, k] = send(
+                z_out.at[k - 1, :, cols],
+                z_in.at[k - 1, :, cols],
+                along(k),
+                z_send.at[p, k - 1],
+                z_recv.at[p, k - 1],
+            )
+
+    hops = [0] + sorted([k for k in order if k > 0], key=lambda k: min(k, outer - k))
+
+    def piece_at(k, x_at, sub_at, p):
+        at = lax.rem(z + outer - k, outer)
+        first = ((at * INNER + x_at) * 2 + sub_at) * width + p * part
+        return out_ref.at[:, pl.ds(pl.multiple_of(first, part), part)]
+
+    along_z = {}
+    along_x = {}
+    across = {}
+    for p, cols in enumerate(parts):
+        summed = totals[n - 1, :, cols] + residual_ref[:, cols].astype(jnp.float32)
+        for k in order:
+            if k > 0:
+                z_copies[p, k].wait_recv()
+                summed = summed + z_in[k - 1, :, cols].astype(jnp.float32)
+        here = piece_at(0, x, sub, p)
+        here[...] = summed.astype(jnp.bfloat16)
+        along_x[p, 0] = send(here, here, other_x, gx_send.at[p, 0], gx_recv.at[p, 0])
+        across[p, 0] = send(here, here, other_core, gs_send.at[p, 0], gs_recv.at[p, 0])
+        for k in hops[1:]:
+            along_z[p, k] = send(
+                here, here, along(k), gz_send.at[p, k - 1], gz_recv.at[p, k - 1]
+            )
+    for p in range(PARTS):
+        for k in hops[1:]:
+            along_z[p, k].wait_recv()
+            piece = piece_at(k, x, sub, p)
+            along_x[p, k] = send(piece, piece, other_x, gx_send.at[p, k], gx_recv.at[p, k])
+            across[p, k] = send(piece, piece, other_core, gs_send.at[p, k], gs_recv.at[p, k])
+    for p in range(PARTS):
         for k in hops:
-            block = block_at(lax.rem(z + outer - k, outer), x_at, 1 - sub)
-            arrived(block, gs_send.at[i * outer + k], gs_recv.at[i * outer + k])
-
+            along_x[p, k].wait_recv()
+            piece = piece_at(k, 1 - x, sub, p)
+            i = outer + k
+            across[p, i] = send(piece, piece, other_core, gs_send.at[p, i], gs_recv.at[p, i])
+    for copy in across.values():
+        copy.wait_recv()
     send_context.wait_send()
-    for copy in send_weight + x_copies + list(z_copies.values()) + sent:
+    for copy in send_weight + sent:
         copy.wait_send()
 
 
@@ -283,16 +285,16 @@
             dma((2 * outer,)),
             dma((2 * outer,)),
             dma((2,)),
-            dma((outer,)),
-            dma((outer,)),
-            dma((outer - 1,)),
-            dma((outer - 1,)),
-            dma((outer - 1,)),
-            dma((outer - 1,)),
-            dma((outer,)),
-            dma((outer,)),
-            dma((2 * outer,)),
-            dma((2 * outer,)),
+            dma((PARTS, outer)),
+            dma((PARTS, outer)),
+            dma((PARTS, outer - 1)),
+            dma((PARTS, outer - 1)),
+            dma((PARTS, outer - 1)),
+            dma((PARTS, outer - 1)),
+            dma((PARTS, outer)),
+            dma((PARTS, outer)),
+            dma((PARTS, 2 * outer)),
+            dma((PARTS, 2 * outer)),
         ],
         compiler_params=pltpu.CompilerParams(
             collective_id=0, has_side_effects=True, vmem_limit_bytes=56 * 2**20
@@ -355,7 +357,7 @@
 def solution(mesh):
     n_tp, n_sub = mesh.shape["tp"], mesh.shape["sub"]
     width = D // (n_tp * n_sub)
-    fused = n_sub == 2 and n_tp % INNER == 0 and 4 <= n_tp <= 16 and width % 128 == 0
+    fused = n_sub == 2 and n_tp % INNER == 0 and 4 <= n_tp <= 16 and width % (128 * PARTS) == 0
     return jax.shard_map(
         per_device_fused if fused else per_device,
         mesh=mesh,

time: 35.7 us -> 32.1 us (0.90)
  Pallas kernels: 33.3 us -> 29.6 us
    pallas_call x1, Pallas kernels: 33.3 us -> 29.6 us  [per_device_fused(): pl.pallas_call(functools.partial(fused_kernel, outer, order), out_shape=j...]
where the time goes in v2:
time: 32.1 us; the launch traced here: 31.9 us
  Pallas kernels  29.6 us (92%)
  local copies, waits for them, and re-layouts  2.26 us (7%)
    pallas_call x1, Pallas kernels, per_device_fused(): pl.pallas_call(functools.partial(fused_kernel, outer, order), out_shape=j...  29.6 us
    unnamed x1, local copies, waits for them, and re-layouts  2.26 us

profile of v2, /device:TPU:0, one launch (start us, length us, event | category | flops | bytes accessed | tf_op | source)
XLA Modules:
  0.0 31.9 jit_solution(605025657625272234)
XLA Ops:
  0.0 29.6 %shard_map.82 = bf16[32,16384]{1,0:T(8,128)(2,1)} custom-call(bf16[16,128]{1,0:T(8,128)(2,1)} %bitcast.7, bf16[16,128]{1,0:T(8,128)(2,1)} %bitcast.8, bf16[16,128]{1,0:T(8,128)(2,1)} %bitcast.9, s32[16]{0:T(128)} %lengths_ref.1, bf16[32,1024]{1,0:T(8,128)(2,1)} %residual_ref.1, bf16[3072,128]{1,0:T(8,128)(2,1)} %bitcast.5, bf16[3072,128]{1,0:T(8,128)(2,1)} %bitcast.6, ...), custom_call_target="tpu_custom_call" | custom-call | tf_op jit(solution)/shard_map/pallas_call | solution.py:266
  29.6 2.3 %copy.10 = bf16[32,16384]{1,0:T(8,128)(2,1)} copy(bf16[32,16384]{1,0:T(8,128)(2,1)} %shard_map.82) | data formatting | bytes 2097152

commit v3 on v2

--- a/solution.py
+++ b/solution.py
@@ -111,6 +111,15 @@
         )
         * scale
     )
+    place = lax.broadcasted_iota(jnp.int32, scores.shape, 1) - row * slots
+    valid = (place >= 0) & (place < filled)
+    scores = jnp.where(valid, scores, -jnp.inf)
+    top = jnp.maximum(jnp.max(scores, axis=1, keepdims=True), own)
+    expo = jnp.exp(scores - top)
+    expo_own = jnp.exp(own - top)
+    total = jnp.sum(expo, axis=1, keepdims=True) + expo_own
+    probs = (expo / total).astype(jnp.bfloat16)
+    probs_own = (expo_own / total).astype(jnp.bfloat16)
     pl.semaphore_wait(barrier, len(partners))
 
     send_weight = []
@@ -126,15 +135,6 @@
         copy.start()
         send_weight.append(copy)
 
-    place = lax.broadcasted_iota(jnp.int32, scores.shape, 1) - row * slots
-    valid = (place >= 0) & (place < filled)
-    scores = jnp.where(valid, scores, -jnp.inf)
-    top = jnp.maximum(jnp.max(scores, axis=1, keepdims=True), own)
-    expo = jnp.exp(scores - top)
-    expo_own = jnp.exp(own - top)
-    total = jnp.sum(expo, axis=1, keepdims=True) + expo_own
-    probs = (expo / total).astype(jnp.bfloat16)
-    probs_own = (expo_own / total).astype(jnp.bfloat16)
     load_values.wait()
     mixed = jnp.dot(probs, values[...], preferred_element_type=jnp.float32)
     mixed = mixed + probs_own.astype(jnp.float32) * value_ref[...].astype(jnp.float32)
@@ -231,18 +231,24 @@
             along_z[p, k] = send(
                 here, here, along(k), gz_send.at[p, k - 1], gz_recv.at[p, k - 1]
             )
-    for p in range(PARTS):
-        for k in hops[1:]:
-            along_z[p, k].wait_recv()
-            piece = piece_at(k, x, sub, p)
-            along_x[p, k] = send(piece, piece, other_x, gx_send.at[p, k], gx_recv.at[p, k])
-            across[p, k] = send(piece, piece, other_core, gs_send.at[p, k], gs_recv.at[p, k])
-    for p in range(PARTS):
+    def from_z(p, k):
+        along_z[p, k].wait_recv()
+        piece = piece_at(k, x, sub, p)
+        along_x[p, k] = send(piece, piece, other_x, gx_send.at[p, k], gx_recv.at[p, k])
+        across[p, k] = send(piece, piece, other_core, gs_send.at[p, k], gs_recv.at[p, k])
+
+    def from_x(p, k):
+        along_x[p, k].wait_recv()
+        piece = piece_at(k, 1 - x, sub, p)
+        i = outer + k
+        across[p, i] = send(piece, piece, other_core, gs_send.at[p, i], gs_recv.at[p, i])
+
+    for p in range(PARTS + 1):
         for k in hops:
-            along_x[p, k].wait_recv()
-            piece = piece_at(k, 1 - x, sub, p)
-            i = outer + k
-            across[p, i] = send(piece, piece, other_core, gs_send.at[p, i], gs_recv.at[p, i])
+            if p < PARTS and k > 0:
+                from_z(p, k)
+            if p > 0:
+                from_x(p - 1, k)
     for copy in across.values():
         copy.wait_recv()
     send_context.wait_send()

time: 32.1 us -> 32.1 us (level)
  no operation moved by 1% of the time
where the time goes in v3:
time: 32.1 us; the launch traced here: 31.9 us
  Pallas kernels  29.6 us (92%)
  local copies, waits for them, and re-layouts  2.26 us (7%)
    pallas_call x1, Pallas kernels, per_device_fused(): pl.pallas_call(functools.partial(fused_kernel, outer, order), out_shape=j...  29.6 us
    unnamed x1, local copies, waits for them, and re-layouts  2.26 us

profile of v3, /device:TPU:0, one launch (start us, length us, event | category | flops | bytes accessed | tf_op | source)
XLA Modules:
  0.0 31.9 jit_solution(18107466028538039560)
XLA Ops:
  0.0 29.6 %shard_map.82 = bf16[32,16384]{1,0:T(8,128)(2,1)} custom-call(bf16[16,128]{1,0:T(8,128)(2,1)} %bitcast.7, bf16[16,128]{1,0:T(8,128)(2,1)} %bitcast.8, bf16[16,128]{1,0:T(8,128)(2,1)} %bitcast.9, s32[16]{0:T(128)} %lengths_ref.1, bf16[32,1024]{1,0:T(8,128)(2,1)} %residual_ref.1, bf16[3072,128]{1,0:T(8,128)(2,1)} %bitcast.5, bf16[3072,128]{1,0:T(8,128)(2,1)} %bitcast.6, ...), custom_call_target="tpu_custom_call" | custom-call | tf_op jit(solution)/shard_map/pallas_call | solution.py:272
  29.6 2.3 %copy.10 = bf16[32,16384]{1,0:T(8,128)(2,1)} copy(bf16[32,16384]{1,0:T(8,128)(2,1)} %shard_map.82) | data formatting | bytes 2097152

commit v4 on v3

--- a/solution.py
+++ b/solution.py
@@ -214,6 +214,11 @@
         first = ((at * INNER + x_at) * 2 + sub_at) * width + p * part
         return out_ref.at[:, pl.ds(pl.multiple_of(first, part), part)]
 
+    def whole_at(k, x_at):
+        at = lax.rem(z + outer - k, outer)
+        first = ((at * INNER + x_at) * 2 + sub) * width
+        return out_ref.at[:, pl.ds(pl.multiple_of(first, width), width)]
+
     along_z = {}
     along_x = {}
     across = {}
@@ -226,7 +231,9 @@
         here = piece_at(0, x, sub, p)
         here[...] = summed.astype(jnp.bfloat16)
         along_x[p, 0] = send(here, here, other_x, gx_send.at[p, 0], gx_recv.at[p, 0])
-        across[p, 0] = send(here, here, other_core, gs_send.at[p, 0], gs_recv.at[p, 0])
+        if p == PARTS - 1:
+            block = whole_at(0, x)
+            across[0] = send(block, block, other_core, gs_send.at[0], gs_recv.at[0])
         for k in hops[1:]:
             along_z[p, k] = send(
                 here, here, along(k), gz_send.at[p, k - 1], gz_recv.at[p, k - 1]
@@ -235,13 +242,16 @@
         along_z[p, k].wait_recv()
         piece = piece_at(k, x, sub, p)
         along_x[p, k] = send(piece, piece, other_x, gx_send.at[p, k], gx_recv.at[p, k])
-        across[p, k] = send(piece, piece, other_core, gs_send.at[p, k], gs_recv.at[p, k])
+        if p == PARTS - 1:
+            block = whole_at(k, x)
+            across[k] = send(block, block, other_core, gs_send.at[k], gs_recv.at[k])
 
     def from_x(p, k):
         along_x[p, k].wait_recv()
-        piece = piece_at(k, 1 - x, sub, p)
-        i = outer + k
-        across[p, i] = send(piece, piece, other_core, gs_send.at[p, i], gs_recv.at[p, i])
+        if p == PARTS - 1:
+            block = whole_at(k, 1 - x)
+            i = outer + k
+            across[i] = send(block, block, other_core, gs_send.at[i], gs_recv.at[i])
 
     for p in range(PARTS + 1):
         for k in hops:
@@ -299,8 +309,8 @@
             dma((PARTS, outer - 1)),
             dma((PARTS, outer)),
             dma((PARTS, outer)),
-            dma((PARTS, 2 * outer)),
-            dma((PARTS, 2 * outer)),
+            dma((2 * outer,)),
+            dma((2 * outer,)),
         ],
         compiler_params=pltpu.CompilerParams(
             collective_id=0, has_side_effects=True, vmem_limit_bytes=56 * 2**20

time: 32.1 us -> 32 us (level)
  no operation moved by 1% of the time
where the time goes in v4:
time: 32 us; the launch traced here: 31.8 us
  Pallas kernels  29.5 us (92%)
  local copies, waits for them, and re-layouts  2.26 us (7%)
    pallas_call x1, Pallas kernels, per_device_fused(): pl.pallas_call(functools.partial(fused_kernel, outer, order), out_shape=j...  29.5 us
    unnamed x1, local copies, waits for them, and re-layouts  2.26 us

profile of v4, /device:TPU:0, one launch (start us, length us, event | category | flops | bytes accessed | tf_op | source)
XLA Modules:
  0.0 31.8 jit_solution(7977079241321532119)
XLA Ops:
  0.0 29.5 %shard_map.82 = bf16[32,16384]{1,0:T(8,128)(2,1)} custom-call(bf16[16,128]{1,0:T(8,128)(2,1)} %bitcast.7, bf16[16,128]{1,0:T(8,128)(2,1)} %bitcast.8, bf16[16,128]{1,0:T(8,128)(2,1)} %bitcast.9, s32[16]{0:T(128)} %lengths_ref.1, bf16[32,1024]{1,0:T(8,128)(2,1)} %residual_ref.1, bf16[3072,128]{1,0:T(8,128)(2,1)} %bitcast.5, bf16[3072,128]{1,0:T(8,128)(2,1)} %bitcast.6, ...), custom_call_target="tpu_custom_call" | custom-call | tf_op jit(solution)/shard_map/pallas_call | solution.py:282
  29.5 2.3 %copy.10 = bf16[32,16384]{1,0:T(8,128)(2,1)} copy(bf16[32,16384]{1,0:T(8,128)(2,1)} %shard_map.82) | data formatting | bytes 2097152
